TPU v7x, 32 devices: a whole 2x2x4 slice. The times are simulated.
32 devices in a mesh: groups: 2 (over x), fsdp: 16 (over z, y, core).
Axes of the slice: x: 2, y: 2, z: 4, core: 2. Of those that a mesh axis runs over, the one named last changes fastest.
Arguments:
- tokens: bfloat16 [32, 128, 4096], P(('groups', 'fsdp')), parts along dimension 0, may hold values from -30 to 30
- cotangent: bfloat16 [32, 128, 4096], P(('groups', 'fsdp')), parts along dimension 0, may hold values from -6 to 6
- block_lang: int32 [32], P('groups'), parts along dimension 0, may hold values from 0 to 3, as said below
- gain: float32 [4096], P('fsdp'), may hold values from 0.1 to 1.9
- w_down: bfloat16 [4096, 4096], P(None, 'fsdp'), may hold values from -0.09375 to 0.09375
- w_up: bfloat16 [4096, 4096], P('fsdp'), may hold values from -0.1875 to 0.1875
Outputs:
- adapted: bfloat16 [32, 128, 4096], P(('groups', 'fsdp')), parts along dimension 0
- x_grad: bfloat16 [32, 128, 4096], P(('groups', 'fsdp')), parts along dimension 0
- grad_down: bfloat16 [8192, 4096], P('groups', 'fsdp'), parts along dimension 0
- grad_up: bfloat16 [8192, 4096], P(('groups', 'fsdp')), parts along dimension 0
- grad_gain: float32 [8192], P(('groups', 'fsdp')), parts along dimension 0
There are 2 independent parts, one for each index of `groups`. A program takes and returns all parts, laid end to end along the dimension named above; an argument that names none is the same for every part. Nothing has to cross between parts.
Inputs may be any that keep to these rules, and one draw needn't show every extreme that they name: `block_lang`: exactly one language, drawn from the seed, labels 6 blocks; the other 3 languages share the remaining 16 - 6 blocks as evenly as possible, their counts differing by at most one.
All inputs are finite; a program needn't handle non-finite values.
Results may differ from a plain program's by a relative error of at most 0.0061.
Values may be sent and summed in bfloat16 or wider, within the bound.
A program may use at most 192 MiB of HBM per device.

v0:
```python
import math

import jax
import jax.numpy as jnp
from jax import lax
from jax.sharding import PartitionSpec as P

OWN = 4
MOSTB = 6


EPSILON = 1e-06


def gelu_tanh(values):
    return jax.nn.gelu(values, approximate=True)


def route_tables(block_lang, languages):
    block_count = block_lang.shape[0]
    onehot = (block_lang[:, None] == jnp.arange(languages, dtype=jnp.int32)[None, :]).astype(
        jnp.int32
    )
    earlier = jnp.cumsum(onehot, axis=0) - onehot
    ranks = jnp.sum(earlier * onehot, axis=1)
    counts = jnp.sum(onehot, axis=0)
    places = jnp.arange(MOSTB, dtype=jnp.int32)
    matches = onehot[:, :, None] * (ranks[:, None, None] == places[None, None, :]).astype(jnp.int32)
    table = jnp.sum(matches * jnp.arange(block_count, dtype=jnp.int32)[:, None, None], axis=0)
    filled = places[None, :] < counts[:, None]
    return (ranks, table, filled)


def pick_rows(rows, table, filled):
    picked = rows[table]
    picked = jnp.where(filled[:, :, None, None], picked, jnp.zeros((), rows.dtype))
    return picked.reshape(table.shape[0], MOSTB * rows.shape[1], rows.shape[2])


def pack_rows(rows, table, filled):
    return jnp.repeat(pick_rows(rows, table, filled), OWN, axis=0)


def dispatch(normed, cotangent, table, filled):
    return (
        lax.all_to_all(
            pack_rows(normed, table, filled), "fsdp", split_axis=0, concat_axis=0, tiled=True
        ),
        lax.all_to_all(
            pack_rows(cotangent, table, filled), "fsdp", split_axis=0, concat_axis=0, tiled=True
        ),
    )


def unpack_rows(sums, block_lang, ranks, per_block):
    shaped = sums.reshape(sums.shape[0], MOSTB, per_block, sums.shape[2])
    return shaped[block_lang, ranks]


def collect(partials, languages):
    returned = lax.all_to_all(partials, "fsdp", split_axis=0, concat_axis=0, tiled=True)
    grouped = returned.reshape(languages, OWN, returned.shape[1], returned.shape[2])
    return jnp.sum(grouped, axis=1, dtype=jnp.float32)


def per_device(tokens, cotangent, block_lang, gain, w_down, w_up):
    devices = lax.axis_size("fsdp")
    languages = devices // OWN
    spread_tok, spread_cot = (
        lax.all_to_all(tokens, "fsdp", split_axis=1, concat_axis=0, tiled=True),
        lax.all_to_all(cotangent, "fsdp", split_axis=1, concat_axis=0, tiled=True),
    )
    block_count, per_block, width = spread_tok.shape
    grad_scale = 1.0 / math.sqrt(block_count * per_block * devices)
    gain_full = lax.all_gather(gain, "fsdp", axis=0, tiled=True)
    ranks, table, filled = route_tables(block_lang, languages)
    wide_rows = spread_tok.astype(jnp.float32)
    root_mean = jnp.sqrt(jnp.mean(wide_rows * wide_rows, axis=-1, keepdims=True) + EPSILON)
    unit_rows = wide_rows / root_mean
    normed = (unit_rows * gain_full).astype(jnp.bfloat16)
    arrived, arrived_cot = dispatch(normed, spread_cot, table, filled)
    rows_in = arrived.reshape(-1, width)
    preact = jnp.dot(rows_in, w_down, preferred_element_type=jnp.float32)
    activ_wide, pullback = jax.vjp(gelu_tanh, preact)
    activation = activ_wide.astype(jnp.bfloat16)
    partial_out = (
        jnp.dot(activation, w_up, preferred_element_type=jnp.float32)
        .astype(jnp.bfloat16)
        .reshape(arrived.shape)
    )
    branch = unpack_rows(collect(partial_out, languages), block_lang, ranks, per_block)
    adapted = (wide_rows + branch).astype(jnp.bfloat16)
    cot_in = arrived_cot.reshape(-1, width)
    upstream = jnp.dot(cot_in, w_up.T, preferred_element_type=jnp.float32)
    dpreact = pullback(upstream)[0].astype(jnp.bfloat16)
    grad_up = (
        jnp.dot(activation.T, cot_in, preferred_element_type=jnp.float32) * grad_scale
    ).astype(jnp.bfloat16)
    grad_down = (
        jnp.dot(rows_in.T, dpreact, preferred_element_type=jnp.float32) * grad_scale
    ).astype(jnp.bfloat16)
    partial_back = (
        jnp.dot(dpreact, w_down.T, preferred_element_type=jnp.float32)
        .astype(jnp.bfloat16)
        .reshape(arrived.shape)
    )
    dnormed = unpack_rows(collect(partial_back, languages), block_lang, ranks, per_block)
    local_gain = jnp.sum(dnormed * unit_rows, axis=(0, 1))
    grad_gain = lax.psum_scatter(local_gain, "fsdp", scatter_dimension=0, tiled=True) * grad_scale
    scaled = dnormed * gain_full
    inner = jnp.mean(scaled * unit_rows, axis=-1, keepdims=True)
    x_grad = (spread_cot.astype(jnp.float32) + (scaled - unit_rows * inner) / root_mean).astype(
        jnp.bfloat16
    )
    adapted_home, x_grad_home = (
        lax.all_to_all(adapted, "fsdp", split_axis=0, concat_axis=1, tiled=True),
        lax.all_to_all(x_grad, "fsdp", split_axis=0, concat_axis=1, tiled=True),
    )
    return (adapted_home, x_grad_home, grad_down, grad_up, grad_gain)


def solution(mesh):
    in_specs = (
        P(("groups", "fsdp"), None, None),
        P(("groups", "fsdp"), None, None),
        P("groups"),
        P("fsdp"),
        P(None, "fsdp"),
        P("fsdp", None),
    )
    out_specs = (
        P(("groups", "fsdp"), None, None),
        P(("groups", "fsdp"), None, None),
        P("groups", "fsdp"),
        P(("groups", "fsdp"), None),
        P(("groups", "fsdp")),
    )
    return jax.shard_map(
        per_device, mesh=mesh, in_specs=in_specs, out_specs=out_specs, check_vma=False
    )
```

profile of v0, /device:TPU:0, one launch (start us, length us, event | category | flops | bytes accessed | tf_op | source)
XLA Modules:
  0.0 829.4 jit_solution(14738390338002280455)
XLA Ops:
  6.2 8.4 %reduce.4 = bf16[128,4096]{1,0:T(8,128)(2,1)S(1)} reduce(bf16[128,1,4096]{2,1,0:T(2,128)(2,1)} %bitcast.95, bf16[]{:T(256)} %broadcast.230), dimensions={1}, to_apply=%bitcast.82.reduce_sub_computation | reduce | bytes 2097154
  16.5 7.6 all-to-all-start
  29.0 9.3 %reduce.3 = bf16[128,4096]{1,0:T(8,128)(2,1)} reduce(bf16[128,1,4096]{2,1,0:T(2,128)(2,1)} %bitcast.96, bf16[]{:T(256)} %broadcast.230), dimensions={1}, to_apply=%bitcast.81.reduce_sub_computation | reduce | bytes 2097154
  41.3 5.7 all-to-all-done
  47.0 6.9 all-to-all-start.4
  55.4 31.9 %all-gather = f32[16,1,256]{2,1,0:T(1,128)S(1)} all-gather(f32[1,1,256]{2,1,0:T(1,128)S(1)} %bitcast.104), channel_id=1, replica_groups=mesh['groups'=2,'fsdp'=16] {'fsdp'}, dimensions={0}, use_global_device_ids=true | all-gather | bytes 17408 | tf_op jit(solution)/shard_map/all_gather | solution.py:75
  94.1 5.8 reshape.247
  114.0 143.0 %all_to_all.65 = bf16[16,48,4096]{2,1,0:T(8,128)(2,1)} all-to-all(bf16[16,48,4096]{2,1,0:T(8,128)(2,1)S(1)} %bitcast.89), channel_id=1, replica_groups=mesh['groups'=2,'fsdp'=16] {'fsdp'}, dimensions={0} | all-to-all | bytes 12582912 | tf_op jit(solution)/shard_map/all_to_all | solution.py:49
  260.3 5.5 all-to-all-start.1
  265.9 6.1 fusion.26
  272.0 108.1 %all-to-all-done.1 = bf16[16,48,4096]{2,1,0:T(8,128)(2,1)} async-done(((bf16[16,48,4096]{2,1,0:T(8,128)(2,1)}), bf16[16,48,4096]{2,1,0:T(8,128)(2,1)}, u32[]{:S(2)}, u32[]{:S(2)}) %all-to-all-start.1) | async-done | bytes 6291488 | tf_op jit(solution)/shard_map/all_to_all | solution.py:46
  380.1 6.0 fusion.15
  390.5 28.5 %all-to-all-start.6 = ((bf16[16,48,4096]{2,1,0:T(8,128)(2,1)}), bf16[16,48,4096]{2,1,0:T(8,128)(2,1)}, u32[]{:S(2)}, u32[]{:S(2)}) async-start(bf16[16,48,4096]{2,1,0:T(8,128)(2,1)} %bitcast.86), calls=%async_computation.6 | async-start | bytes 12582912 | tf_op jit(solution)/shard_map/all_to_all | solution.py:61
  419.0 6.1 convolution_convert_fusion.1
  425.1 108.1 %all-to-all-done.6 = bf16[16,48,4096]{2,1,0:T(8,128)(2,1)} async-done(((bf16[16,48,4096]{2,1,0:T(8,128)(2,1)}), bf16[16,48,4096]{2,1,0:T(8,128)(2,1)}, u32[]{:S(2)}, u32[]{:S(2)}) %all-to-all-start.6) | async-done | bytes 6291488 | tf_op jit(solution)/shard_map/all_to_all | solution.py:61
  533.2 28.2 %all-to-all-start.2 = ((bf16[16,48,4096]{2,1,0:T(8,128)(2,1)}), bf16[16,48,4096]{2,1,0:T(8,128)(2,1)}, u32[]{:S(2)}, u32[]{:S(2)}) async-start(bf16[16,48,4096]{2,1,0:T(8,128)(2,1)} %bitcast.87), calls=%async_computation.2 | async-start | bytes 12582912 | tf_op jit(solution)/shard_map/all_to_all | solution.py:61
  561.5 5.9 convert_reduce_fusion
  572.7 102.9 %all-to-all-done.2 = bf16[16,48,4096]{2,1,0:T(8,128)(2,1)} async-done(((bf16[16,48,4096]{2,1,0:T(8,128)(2,1)}), bf16[16,48,4096]{2,1,0:T(8,128)(2,1)}, u32[]{:S(2)}, u32[]{:S(2)}) %all-to-all-start.2) | async-done | bytes 6291488 | tf_op jit(solution)/shard_map/all_to_all | solution.py:61
  675.7 6.0 convert_reduce_fusion.1
  685.7 5.5 add_convert_fusion
  691.2 52.8 %all_to_all.66 = bf16[16,8,4096]{2,1,0:T(8,128)(2,1)S(1)} all-to-all(bf16[16,8,4096]{2,1,0:T(8,128)(2,1)S(1)} %get-tuple-element.11), channel_id=1, replica_groups=mesh['groups'=2,'fsdp'=16] {'fsdp'}, dimensions={0} | all-to-all | bytes 2097152 | tf_op jit(solution)/shard_map/all_to_all | solution.py:117
  750.7 6.1 fusion.1
  756.7 6.0 fusion
  762.7 62.2 %all-reduce = f32[4096]{0:T(1024)S(1)} all-reduce(f32[4096]{0:T(1024)S(1)} %copy-done.7), channel_id=2, replica_groups=mesh['groups'=2,'fsdp'=16] {'fsdp'}, use_global_device_ids=true, to_apply=%region_9.10.clone | all-reduce | flops 4096 | bytes 32768
  (71 shorter events, 64.9 us)
Async XLA Ops:
  0.6 379.5 %copy-start = (bf16[4096,256]{1,0:T(8,128)(2,1)S(1)}, bf16[4096,256]{1,0:T(8,128)(2,1)}, u32[]{:S(2)}) copy-start(bf16[4096,256]{1,0:T(8,128)(2,1)} %param.10) | copy-start | bytes 6291460
  16.5 30.5 %all-to-all-start = ((bf16[16,2,16384]{2,1,0:T(2,128)(2,1)}), bf16[16,2,16384]{2,1,0:T(2,128)(2,1)S(1)}, u32[]{:S(2)}, u32[]{:S(2)}) async-start(bf16[16,2,16384]{2,1,0:T(2,128)(2,1)} %reshape.244), calls=%async_computation | async-start | bytes 2097152 | tf_op jit(solution)/shard_map/all_to_all | solution.py:70
  38.3 15.6 %copy-start.8 = (s32[16]{0:T(128)S(1)}, s32[16]{0:T(128)}, u32[]{:S(2)}) copy-start(s32[16]{0:T(128)} %param.8) | copy-start | bytes 196
  38.4 17.1 %copy-start.12 = (f32[256]{0:T(256)S(1)}, f32[256]{0:T(256)}, u32[]{:S(2)}) copy-start(f32[256]{0:T(256)} %param.9) | copy-start | bytes 3076
  47.0 47.1 %all-to-all-start.4 = ((bf16[16,2,16384]{2,1,0:T(2,128)(2,1)}), bf16[16,2,16384]{2,1,0:T(2,128)(2,1)}, u32[]{:S(2)}, u32[]{:S(2)}) async-start(bf16[16,2,16384]{2,1,0:T(2,128)(2,1)} %reshape.246), calls=%async_computation.4 | async-start | bytes 2097152 | tf_op jit(solution)/shard_map/all_to_all | solution.py:71
  54.3 0.5 copy-start.10
  87.4 16.2 %copy-start.6 = (f32[16,1,256]{2,1,0:T(1,128)}, f32[16,1,256]{2,1,0:T(1,128)S(1)}, u32[]{:S(2)}) copy-start(f32[16,1,256]{2,1,0:T(1,128)S(1)} %all-gather) | copy-start | bytes 49156
  260.3 119.7 %all-to-all-start.1 = ((bf16[16,48,4096]{2,1,0:T(8,128)(2,1)}), bf16[16,48,4096]{2,1,0:T(8,128)(2,1)}, u32[]{:S(2)}, u32[]{:S(2)}) async-start(bf16[16,48,4096]{2,1,0:T(8,128)(2,1)} %bitcast.88), calls=%async_computation.1 | async-start | bytes 12582912 | tf_op jit(solution)/shard_map/all_to_all | solution.py:46
  390.5 28.5 %copy-start.4 = (f32[768,256]{1,0:T(8,128)S(1)}, f32[768,256]{1,0:T(8,128)}, u32[]{:S(2)}) copy-start(f32[768,256]{1,0:T(8,128)} %get-tuple-element.16) | copy-start | bytes 2359300
  390.5 142.7 %all-to-all-start.6 = ((bf16[16,48,4096]{2,1,0:T(8,128)(2,1)}), bf16[16,48,4096]{2,1,0:T(8,128)(2,1)}, u32[]{:S(2)}, u32[]{:S(2)}) async-start(bf16[16,48,4096]{2,1,0:T(8,128)(2,1)} %bitcast.86), calls=%async_computation.6 | async-start | bytes 12582912 | tf_op jit(solution)/shard_map/all_to_all | solution.py:61
  533.2 28.2 %copy-start.9 = (s32[16]{0:T(128)S(1)}, s32[16]{0:T(128)}, u32[]{:S(2)}) copy-start(s32[16]{0:T(128)} %param.8) | copy-start | bytes 196
  533.2 28.3 %copy-start.11 = (s32[16]{0:T(128)S(1)}, s32[16]{0:T(128)}, u32[]{:S(2)}) copy-start(s32[16]{0:T(128)} %copy-done.10) | copy-start | bytes 196
  533.2 142.4 %all-to-all-start.2 = ((bf16[16,48,4096]{2,1,0:T(8,128)(2,1)}), bf16[16,48,4096]{2,1,0:T(8,128)(2,1)}, u32[]{:S(2)}, u32[]{:S(2)}) async-start(bf16[16,48,4096]{2,1,0:T(8,128)(2,1)} %bitcast.87), calls=%async_computation.2 | async-start | bytes 12582912 | tf_op jit(solution)/shard_map/all_to_all | solution.py:61
  570.0 111.6 %copy-start.3 = (f32[16,8,4096]{2,1,0:T(8,128)}, f32[16,8,4096]{2,1,0:T(8,128)S(1)}, u32[]{:S(2)}) copy-start(f32[16,8,4096]{2,1,0:T(8,128)S(1)} %gather_fusion.3) | copy-start | bytes 6291460
  681.6 4.1 copy-start.2
  691.2 58.2 %copy-start.13 = (u32[32]{0:T(128)S(1)}, u32[32]{0:T(128)}, u32[]{:S(2)}) copy-start(u32[32]{0:T(128)} %constant.70) | copy-start | bytes 388
  691.2 59.4 %copy-start.5 = (f32[768,256]{1,0:T(8,128)S(1)}, f32[768,256]{1,0:T(8,128)}, u32[]{:S(2)}) copy-start(f32[768,256]{1,0:T(8,128)} %get-tuple-element.16) | copy-start | bytes 2359300
  744.0 81.5 %all-to-all-start.3 = ((bf16[16,8,4096]{2,1,0:T(8,128)(2,1)}), bf16[16,8,4096]{2,1,0:T(8,128)(2,1)}, u32[]{:S(2)}, u32[]{:S(2)}) async-start(bf16[16,8,4096]{2,1,0:T(8,128)(2,1)} %get-tuple-element.12), calls=%async_computation.3 | async-start | bytes 2097152 | tf_op jit(solution)/shard_map/all_to_all | solution.py:116
  756.7 6.0 copy-start.7
  825.5 3.4 copy-start.1
where the time goes:
time: 837 us; the launch traced here: 829 us
  waiting for transfers between devices  325 us (39%)
  blocking collectives  290 us (35%)
  starting transfers between devices  82.1 us (10%)
  local copies, waits for them, and re-layouts  51 us (6%)
  other arithmetic  45 us (5%)
  matrix products  34.7 us (4%)
    all_to_all x2, waiting for transfers between devices, collect(): lax.all_to_all(partials, 'fsdp', split_axis=0, concat_axis=0, tiled=True)  211 us
    all_to_all x1, blocking collectives, dispatch(): lax.all_to_all(pack_rows(cotangent, table, filled), 'fsdp', split_axis=0,...  143 us
    all_to_all x1, waiting for transfers between devices, dispatch(): lax.all_to_all(pack_rows(normed, table, filled), 'fsdp', split_axis=0, co...  108 us
    unnamed x1, blocking collectives  62.2 us
    all_to_all x2, starting transfers between devices, collect(): lax.all_to_all(partials, 'fsdp', split_axis=0, concat_axis=0, tiled=True)  56.7 us
    all_to_all x1, blocking collectives, per_device(): lax.all_to_all(x_grad, 'fsdp', split_axis=0, concat_axis=1, tiled=True)  52.8 us
    unnamed x39, local copies, waits for them, and re-layouts  32.8 us
    all_gather x1, blocking collectives, per_device(): gain_full = lax.all_gather(gain, 'fsdp', axis=0, tiled=True)  31.9 us
  transfers between devices with their start and end apart: 6, of which 4 were waited for; matrix products, arithmetic and copies ran while one was open for 7% of the time, Pallas kernels for 0%

commit v1 on v0

v1 whole, which is shorter than its diff:
```python
import functools
import math

import jax
import jax.numpy as jnp
from jax import lax
from jax.experimental import pallas as pl
from jax.experimental.pallas import tpu as pltpu
from jax.sharding import PartitionSpec as P

OWN = 4
MOSTB = 6
EPSILON = 1e-06
ANY = pl.BlockSpec(memory_space=pl.ANY)


def gelu_tanh(values):
    return jax.nn.gelu(values, approximate=True)


def route_tables(block_lang, languages):
    block_count = block_lang.shape[0]
    onehot = (block_lang[:, None] == jnp.arange(languages, dtype=jnp.int32)[None, :]).astype(
        jnp.int32
    )
    earlier = jnp.cumsum(onehot, axis=0) - onehot
    ranks = jnp.sum(earlier * onehot, axis=1)
    counts = jnp.sum(onehot, axis=0)
    places = jnp.arange(MOSTB, dtype=jnp.int32)
    matches = onehot[:, :, None] * (ranks[:, None, None] == places[None, None, :]).astype(jnp.int32)
    table = jnp.sum(matches * jnp.arange(block_count, dtype=jnp.int32)[:, None, None], axis=0)
    filled = places[None, :] < counts[:, None]
    return (ranks, table, filled)


def peer_of(kind, me, step, devices):
    if kind == "all":
        return lax.rem(me + step, devices)
    if kind == "across":
        return lax.rem(me + step * OWN, devices)
    return (me // OWN) * OWN + lax.rem(lax.rem(me, OWN) + step, OWN)


def size_of(kind, devices):
    return {"all": devices, "across": devices // OWN, "owners": OWN}[kind]


def exchange_kernel(devices, plans, n_in, n_out, *refs):
    ins, outs = refs[:n_in], refs[n_in : n_in + n_out]
    sems = refs[n_in + n_out :]
    me = lax.axis_index("fsdp")
    barrier = pltpu.get_barrier_semaphore()
    total = 0
    for kind, _ in plans:

        def greet(step, carry, kind=kind):
            pl.semaphore_signal(
                barrier,
                inc=1,
                device_id={"fsdp": peer_of(kind, me, step, devices)},
                device_id_type=pl.DeviceIdType.MESH,
            )
            return carry

        lax.fori_loop(1, size_of(kind, devices), greet, 0)
        total += size_of(kind, devices) - 1
    pl.semaphore_wait(barrier, total)

    def remote(at, index, step):
        kind, moves = plans[at]
        send, recv, _ = sems[3 * at : 3 * at + 3]
        source, take, target, put = moves[index]
        peer = peer_of(kind, me, step, devices)
        return pltpu.make_async_remote_copy(
            src_ref=take(ins[source], peer),
            dst_ref=put(outs[target], me),
            send_sem=send.at[index, step],
            recv_sem=recv.at[index, step],
            device_id={"fsdp": peer},
            device_id_type=pl.DeviceIdType.MESH,
        )

    def local(at, index):
        source, take, target, put = plans[at][1][index]
        own = sems[3 * at + 2]
        return pltpu.make_async_copy(take(ins[source], me), put(outs[target], me), own.at[index])

    for at, (kind, moves) in enumerate(plans):

        def begin(step, carry, at=at, moves=moves):
            for index in range(len(moves)):
                remote(at, index, step).start()
            return carry

        lax.fori_loop(1, size_of(kind, devices), begin, 0)
        for index in range(len(moves)):
            local(at, index).start()
    for at, (kind, moves) in enumerate(plans):

        def finish(step, carry, at=at, moves=moves):
            for index in range(len(moves)):
                remote(at, index, step).wait()
            return carry

        lax.fori_loop(1, size_of(kind, devices), finish, 0)
        for index in range(len(moves)):
            local(at, index).wait()


def exchange(devices, collective_id, plans, inputs, out_shapes):
    scratch = []
    for kind, moves in plans:
        count = size_of(kind, devices)
        scratch += [
            pltpu.SemaphoreType.DMA((len(moves), count)),
            pltpu.SemaphoreType.DMA((len(moves), count)),
            pltpu.SemaphoreType.DMA((len(moves),)),
        ]
    return pl.pallas_call(
        functools.partial(exchange_kernel, devices, plans, len(inputs), len(out_shapes)),
        out_shape=[jax.ShapeDtypeStruct(shape, dtype) for shape, dtype in out_shapes],
        in_specs=[ANY] * len(inputs),
        out_specs=[ANY] * len(out_shapes),
        scratch_shapes=scratch,
        compiler_params=pltpu.CompilerParams(
            collective_id=collective_id, has_side_effects=True
        ),
    )(*inputs)


def span(index, width):
    return pl.ds(pl.multiple_of(index * width, width), width)


def per_device(tokens, cotangent, block_lang, gain, w_down, w_up):
    bf16, f32 = jnp.bfloat16, jnp.float32
    devices = lax.axis_size("fsdp")
    languages = devices // OWN
    per_block, width = tokens.shape[1:]
    rows = per_block // languages
    quarter = width // OWN
    units = w_down.shape[1]
    hidden = units * OWN
    gain_width = gain.shape[0]
    slots = languages * MOSTB * rows
    grad_scale = 1.0 / math.sqrt(devices * per_block)
    me = lax.axis_index("fsdp")
    rank_here = lax.rem(me, OWN)

    ranks, table, filled = route_tables(block_lang, languages)
    home = tokens.reshape(per_block, width).astype(f32)
    home_cot = cotangent.reshape(per_block, width)
    root_mean = jnp.sqrt(jnp.mean(home * home, axis=-1, keepdims=True) + EPSILON)

    def slab(ref, peer):
        return ref.at[peer // OWN, :, span(lax.rem(peer, OWN), quarter)]

    def whole(ref, peer):
        return ref.at[0]

    def piece(ref, peer):
        return ref.at[peer // OWN]

    def at_device(ref, me):
        return ref.at[me]

    spread_tok, spread_cot, spread_root, gain_all = exchange(
        devices,
        1,
        [
            (
                "all",
                [
                    (2, piece, 2, at_device),
                    (3, whole, 3, at_device),
                    (0, slab, 0, at_device),
                    (1, slab, 1, at_device),
                ],
            )
        ],
        [
            tokens.reshape(languages, rows, width),
            cotangent.reshape(languages, rows, width),
            jnp.broadcast_to(root_mean, (per_block, 128)).reshape(languages, rows, 128),
            jnp.broadcast_to(gain, (1, 8, gain_width)),
        ],
        [
            ((devices, rows, quarter), bf16),
            ((devices, rows, quarter), bf16),
            ((devices, rows, 128), f32),
            ((devices, 8, gain_width), f32),
        ],
    )
    gain_full = gain_all[:, 0, :].reshape(width)
    gain_here = lax.dynamic_slice_in_dim(gain_full, rank_here * quarter, quarter)
    unit_rows = spread_tok.astype(f32) / spread_root[:, :, :1]
    normed = (unit_rows * gain_here).astype(bf16)

    def pick(values):
        return jnp.where(filled[:, :, None, None], values[table], jnp.zeros((), bf16))

    def at_place(ref, me):
        return ref.at[me // OWN]

    rows_in, cot_in, down, up = exchange(
        devices,
        2,
        [
            ("across", [(0, piece, 0, at_place), (1, piece, 1, at_place)]),
            (
                "owners",
                [
                    (
                        2,
                        lambda ref, peer: ref.at[span(lax.rem(peer, OWN), quarter), :],
                        2,
                        lambda ref, me: ref.at[:, span(lax.rem(me, OWN), units)],
                    ),
                    (
                        3,
                        lambda ref, peer: ref.at[:, span(lax.rem(peer, OWN), quarter)],
                        3,
                        lambda ref, me: ref.at[span(lax.rem(me, OWN), units), :],
                    ),
                ],
            ),
        ],
        [pick(normed), pick(spread_cot), w_down, w_up],
        [
            ((languages, MOSTB, rows, quarter), bf16),
            ((languages, MOSTB, rows, quarter), bf16),
            ((quarter, hidden), bf16),
            ((hidden, quarter), bf16),
        ],
    )
    rows_in = rows_in.reshape(slots, quarter)
    cot_in = cot_in.reshape(slots, quarter)

    part_pre = jnp.dot(rows_in, down, preferred_element_type=f32).astype(bf16)
    part_up = jnp.dot(cot_in, up.T, preferred_element_type=f32).astype(bf16)

    def unit_span(ref, peer):
        return ref.at[:, span(lax.rem(peer, OWN), units)]

    def at_rank(ref, me):
        return ref.at[lax.rem(me, OWN)]

    pre_parts, up_parts = exchange(
        devices,
        3,
        [("owners", [(0, unit_span, 0, at_rank), (1, unit_span, 1, at_rank)])],
        [part_pre, part_up],
        [((OWN, slots, units), bf16), ((OWN, slots, units), bf16)],
    )
    preact = jnp.sum(pre_parts, axis=0, dtype=f32)
    upstream = jnp.sum(up_parts, axis=0, dtype=f32)
    activ_wide, pullback = jax.vjp(gelu_tanh, preact)
    dpreact_here = pullback(upstream)[0].astype(bf16)

    def all_of(ref, peer):
        return ref

    activation, dpreact = exchange(
        devices,
        4,
        [("owners", [(0, all_of, 0, unit_span), (1, all_of, 1, unit_span)])],
        [activ_wide.astype(bf16), dpreact_here],
        [((slots, hidden), bf16), ((slots, hidden), bf16)],
    )
    shape = (languages, MOSTB, rows, quarter)
    out = jnp.dot(activation, up, preferred_element_type=f32).astype(bf16).reshape(shape)
    back = jnp.dot(dpreact, down.T, preferred_element_type=f32).astype(bf16).reshape(shape)
    part_grad_up = (
        jnp.dot(activation.T, cot_in, preferred_element_type=f32) * grad_scale
    ).astype(bf16)
    part_grad_down = (
        jnp.dot(rows_in.T, dpreact, preferred_element_type=f32) * grad_scale
    ).astype(bf16)

    out_home, back_home, grad_down, grad_up = exchange(
        devices,
        5,
        [
            ("across", [(0, piece, 0, at_place), (1, piece, 1, at_place)]),
            (
                "owners",
                [
                    (
                        2,
                        unit_span,
                        2,
                        lambda ref, me: ref.at[span(lax.rem(me, OWN), quarter), :],
                    ),
                    (
                        3,
                        lambda ref, peer: ref.at[span(lax.rem(peer, OWN), units), :],
                        3,
                        lambda ref, me: ref.at[:, span(lax.rem(me, OWN), quarter)],
                    ),
                ],
            ),
        ],
        [out, back, part_grad_down, part_grad_up],
        [(shape, bf16), (shape, bf16), ((width, units), bf16), ((units, width), bf16)],
    )
    branch_rows = out_home[block_lang, ranks]
    dnormed_rows = back_home[block_lang, ranks]
    gain_part = jnp.sum(dnormed_rows.astype(f32) * unit_rows, axis=(0, 1))

    def at_home(ref, me):
        return ref.at[me // OWN, :, span(lax.rem(me, OWN), quarter)]

    branch, dnormed, gain_parts = exchange(
        devices,
        6,
        [
            (
                "all",
                [
                    (2, lambda ref, peer: ref.at[lax.rem(peer, languages)], 2, at_device),
                    (0, at_device, 0, at_home),
                    (1, at_device, 1, at_home),
                ],
            )
        ],
        [
            branch_rows,
            dnormed_rows,
            jnp.broadcast_to(
                gain_part.reshape(languages, 1, gain_width), (languages, 8, gain_width)
            ),
        ],
        [
            ((languages, rows, width), bf16),
            ((languages, rows, width), bf16),
            ((devices, 8, gain_width), f32),
        ],
    )
    holders = gain_parts[:, 0, :].reshape(languages, OWN, gain_width)
    grad_gain = (
        jnp.sum(
            lax.dynamic_index_in_dim(holders, me // languages, axis=1, keepdims=False), axis=0
        )
        * grad_scale
    )
    adapted = (home + branch.reshape(per_block, width).astype(f32)).astype(bf16)
    unit = home / root_mean
    scaled = dnormed.reshape(per_block, width).astype(f32) * gain_full
    inner = jnp.mean(scaled * unit, axis=-1, keepdims=True)
    x_grad = (home_cot.astype(f32) + (scaled - unit * inner) / root_mean).astype(bf16)
    return (
        adapted.reshape(tokens.shape),
        x_grad.reshape(tokens.shape),
        grad_down,
        grad_up,
        grad_gain,
    )


def solution(mesh):
    in_specs = (
        P(("groups", "fsdp"), None, None),
        P(("groups", "fsdp"), None, None),
        P("groups"),
        P("fsdp"),
        P(None, "fsdp"),
        P("fsdp", None),
    )
    out_specs = (
        P(("groups", "fsdp"), None, None),
        P(("groups", "fsdp"), None, None),
        P("groups", "fsdp"),
        P(("groups", "fsdp"), None),
        P(("groups", "fsdp")),
    )
    return jax.shard_map(
        per_device, mesh=mesh, in_specs=in_specs, out_specs=out_specs, check_vma=False
    )
```

time: 837 us -> 387 us (0.46)
  the two profiles are of different devices: /device:TPU:0 before, /device:TPU:13 now
where the time goes in v1:
time: 387 us
  Pallas kernels  328 us (85%)
  matrix products  22.1 us (6%)
  local copies, waits for them, and re-layouts  17.9 us (5%)
  other arithmetic  17.2 us (4%)
    pallas_call x6, Pallas kernels, exchange(): pl.pallas_call(functools.partial(exchange_kernel, devices, plans, len(inp...  328 us

profile of v1, /device:TPU:13, one launch (start us, length us, event | category | flops | bytes accessed | tf_op | source)
XLA Modules:
  0.0 386.6 jit_solution(1308579559180252116)
XLA Ops:
  0.7 1.5 fusion
  7.1 60.0 %shard_map.101 = (bf16[16,32,1024]{2,1,0:T(8,128)(2,1)}, bf16[16,32,1024]{2,1,0:T(8,128)(2,1)}, f32[16,32,128]{2,1,0:T(8,128)}, f32[16,8,256]{2,1,0:T(8,128)}) custom-call(bf16[4,32,4096]{2,1,0:T(8,128)(2,1)} %bitcast.47, bf16[4,32,4096]{2,1,0:T(8,128)(2,1)} %bitcast.52, f32[4,32,128]{2,1,0:T(8,128)} %broadcast_in_dim.27.refs_2_, ...), custom_call_target="tpu_custom_call" | custom-call | tf_op jit(solution)/shard_map/pallas_call | solution.py:119
  69.1 1.6 multiply_convert_fusion.2
  71.4 1.9 gather_fusion.1
  73.3 1.9 broadcast_select_fusion
  75.2 69.8 %shard_map.102 = (bf16[4,6,32,1024]{3,2,1,0:T(8,128)(2,1)}, bf16[4,6,32,1024]{3,2,1,0:T(8,128)(2,1)}, bf16[1024,1024]{1,0:T(8,128)(2,1)}, bf16[1024,1024]{1,0:T(8,128)(2,1)}) custom-call(bf16[4,6,32,1024]{3,2,1,0:T(8,128)(2,1)} %get-tuple-element.50.refs_0_, bf16[4,6,32,1024]{3,2,1,0:T(8,128)(2,1)} %get-tuple-element.49.refs_1_, bf16[4096,256]{1,0:T(8,128)(2,1)} %refs_2_.1, ...), custom_call_target="tpu_custom_call" | custom-call | tf_op jit(solution)/shard_map/pallas_call | solution.py:119
  145.1 5.2 %convolution_convert_fusion.2.refs_1_ = bf16[768,1024]{1,0:T(8,128)(2,1)} fusion(bf16[768,1024]{1,0:T(8,128)(2,1)} %bitcast.61, bf16[1024,1024]{1,0:T(8,128)(2,1)} %get-tuple-element.31), kind=kOutput, calls=%fused_computation.25 | convolution fusion | flops 1611399168 | bytes 5242880 | tf_op jit(solution)/shard_map/dot_general | solution.py:240
  150.3 3.0 convolution_convert_fusion.3.refs_0_
  153.2 36.6 %shard_map.103 = (bf16[4,768,256]{2,1,0:T(8,128)(2,1)}, bf16[4,768,256]{2,1,0:T(8,128)(2,1)}) custom-call(bf16[768,1024]{1,0:T(8,128)(2,1)} %convolution_convert_fusion.3.refs_0_, bf16[768,1024]{1,0:T(8,128)(2,1)} %convolution_convert_fusion.2.refs_1_), custom_call_target="tpu_custom_call" | custom-call | tf_op jit(solution)/shard_map/pallas_call | solution.py:119
  189.9 2.5 convert_reduce_fusion
  192.4 1.4 fusion.13
  193.8 36.6 %shard_map.104 = (bf16[768,1024]{1,0:T(8,128)(2,1)}, bf16[768,1024]{1,0:T(8,128)(2,1)}) custom-call(bf16[768,256]{1,0:T(8,128)(2,1)} %get-tuple-element.48.refs_0_, bf16[768,256]{1,0:T(8,128)(2,1)} %get-tuple-element.47.refs_1_), custom_call_target="tpu_custom_call" | custom-call | tf_op jit(solution)/shard_map/pallas_call | solution.py:119
  230.5 4.7 %convolution_convert_fusion = bf16[768,1024]{1,0:T(8,128)(2,1)} fusion(bf16[768,1024]{1,0:T(8,128)(2,1)} %get-tuple-element.35, bf16[1024,1024]{1,0:T(8,128)(2,1)S(1)} %copy-done.9), kind=kOutput, calls=%fused_computation.23 | convolution fusion | flops 1611399168 | bytes 5242880 | tf_op jit(solution)/shard_map/dot_general | solution.py:272
  235.2 3.0 convolution_convert_fusion.1
  238.2 3.2 multiply_convert_fusion.refs_3_
  241.3 3.2 multiply_convert_fusion.1.refs_2_
  244.5 71.6 %shard_map.105 = (bf16[4,6,32,1024]{3,2,1,0:T(8,128)(2,1)}, bf16[4,6,32,1024]{3,2,1,0:T(8,128)(2,1)}, bf16[4096,256]{1,0:T(8,128)(2,1)}, bf16[256,4096]{1,0:T(8,128)(2,1)}) custom-call(bf16[4,6,32,1024]{3,2,1,0:T(8,128)(2,1)} %bitcast.54, bf16[4,6,32,1024]{3,2,1,0:T(8,128)(2,1)} %bitcast.53, bf16[1024,1024]{1,0:T(8,128)(2,1)} %multiply_convert_fusion.1.refs_2_, ...), custom_call_target="tpu_custom_call" | custom-call | tf_op jit(solution)/shard_map/pallas_call | solution.py:119
  316.1 3.1 gather_fusion.2
  319.2 2.0 gather_fusion.3
  322.5 53.9 %shard_map.106 = (bf16[4,32,4096]{2,1,0:T(8,128)(2,1)}, bf16[4,32,4096]{2,1,0:T(8,128)(2,1)}, f32[16,8,256]{2,1,0:T(8,128)}) custom-call(bf16[16,32,1024]{2,1,0:T(8,128)(2,1)} %gather_fusion.2, bf16[16,32,1024]{2,1,0:T(8,128)(2,1)} %copy-done.1, f32[4,8,256]{2,1,0:T(8,128)} %broadcast_in_dim.32.refs_2_), custom_call_target="tpu_custom_call" | custom-call | tf_op jit(solution)/shard_map/pallas_call | solution.py:119
  376.4 1.9 multiply_reduce_fusion
  380.6 2.3 fusion.6
  382.9 1.3 copy.16
  385.3 1.3 copy.17
  (60 shorter events, 12.2 us)
Async XLA Ops:
  145.1 5.2 %copy-start.9 = (bf16[1024,1024]{1,0:T(8,128)(2,1)S(1)}, bf16[1024,1024]{1,0:T(8,128)(2,1)}, u32[]{:S(2)}) copy-start(bf16[1024,1024]{1,0:T(8,128)(2,1)} %get-tuple-element.29) | copy-start | bytes 6291460
  145.1 5.2 %copy-start.10 = (bf16[4,6,32,1024]{3,2,1,0:T(8,128)(2,1)S(1)}, bf16[4,6,32,1024]{3,2,1,0:T(8,128)(2,1)}, u32[]{:S(2)}) copy-start(bf16[4,6,32,1024]{3,2,1,0:T(8,128)(2,1)} %get-tuple-element.28) | copy-start | bytes 4718596
  230.5 4.7 %copy-start.8 = (bf16[1024,1024]{1,0:T(8,128)(2,1)S(1)}, bf16[1024,1024]{1,0:T(8,128)(2,1)}, u32[]{:S(2)}) copy-start(bf16[1024,1024]{1,0:T(8,128)(2,1)} %get-tuple-element.31) | copy-start | bytes 6291460
  230.5 4.7 %copy-start.14 = (bf16[768,1024]{1,0:T(8,128)(2,1)S(1)}, bf16[768,1024]{1,0:T(8,128)(2,1)}, u32[]{:S(2)}) copy-start(bf16[768,1024]{1,0:T(8,128)(2,1)} %get-tuple-element.34) | copy-start | bytes 4718596
  235.2 3.0 copy-start.12
  238.2 3.2 copy-start.11
  238.2 3.2 copy-start.13
  316.1 5.1 %copy-start.3 = (bf16[16,32,1024]{2,1,0:T(8,128)(2,1)S(1)}, bf16[16,32,1024]{2,1,0:T(8,128)(2,1)}, u32[]{:S(2)}) copy-start(bf16[16,32,1024]{2,1,0:T(8,128)(2,1)} %get-tuple-element.24) | copy-start | bytes 3145732
  321.2 1.3 copy-start.1
  321.2 55.2 %copy-start = (bf16[1,128,4096]{2,1,0:T(8,128)(2,1)S(1)}, bf16[1,128,4096]{2,1,0:T(8,128)(2,1)}, u32[]{:S(2)}) copy-start(bf16[1,128,4096]{2,1,0:T(8,128)(2,1)} %param.6) | copy-start | bytes 3145732
  376.4 3.6 copy-start.2
  378.2 1.9 copy-start.4
  379.4 1.3 copy-start.7
  380.6 2.3 copy-start.6
  382.9 2.3 copy-start.5

commit v2 on v1

--- a/solution.py
+++ b/solution.py
@@ -132,6 +132,276 @@
     return pl.ds(pl.multiple_of(index * width, width), width)
 
 
+ROW_TILE = 256
+TRANSFERS = 12
+TOK, COT, DOWN, UP, PRE, UPS, ACT, DPRE, OUT, BACK, GUP, GDOWN = range(TRANSFERS)
+GELU_C = math.sqrt(2.0 / math.pi)
+
+
+def adapter_kernel(
+    devices, grad_scale, tok_ref, cot_ref, wd_ref, wu_ref, out_ref, back_ref, gd_ref, gu_ref,
+    rows, cots, down, up, pre_out, pre_in, ups_out, ups_in, act, dpre, slope, out, back, gup, gdown,
+    send, recv, own,
+):
+    bf16, f32 = jnp.bfloat16, jnp.float32
+    me = lax.axis_index("fsdp")
+    group, rank = me // OWN, lax.rem(me, OWN)
+    languages = devices // OWN
+    slots, quarter = rows.shape
+    chunk = slots // languages
+    units = wd_ref.shape[1]
+    wide = min(512, quarter)
+    tiles = slots // ROW_TILE
+
+    barrier = pltpu.get_barrier_semaphore()
+    for kind in ("across", "owners"):
+
+        def greet(step, carry, kind=kind):
+            pl.semaphore_signal(
+                barrier,
+                inc=1,
+                device_id={"fsdp": peer_of(kind, me, step, devices)},
+                device_id_type=pl.DeviceIdType.MESH,
+            )
+            return carry
+
+        lax.fori_loop(1, size_of(kind, devices), greet, 0)
+    pl.semaphore_wait(barrier, languages - 1 + OWN - 1)
+
+    def group_rows(ref):
+        return lambda device, step: ref.at[span(device // OWN, chunk), :]
+
+    def feature_rows(ref):
+        return lambda device, step: ref.at[span(lax.rem(device, OWN), quarter), :]
+
+    def feature_columns(ref):
+        return lambda device, step: ref.at[:, span(lax.rem(device, OWN), quarter)]
+
+    def unit_rows(ref):
+        return lambda device, step: ref.at[span(lax.rem(device, OWN), units), :]
+
+    def unit_columns(ref):
+        return lambda device, step: ref.at[:, span(lax.rem(device, OWN), units)]
+
+    def by_rank(ref):
+        return lambda device, step: ref.at[lax.rem(device, OWN)]
+
+    def by_step(ref):
+        return lambda device, step: ref.at[step - 1]
+
+    def mine(ref):
+        return lambda device, step: ref.at[rank]
+
+    moves = {
+        TOK: ("across", group_rows(tok_ref), group_rows(rows), True),
+        COT: ("across", group_rows(cot_ref), group_rows(cots), True),
+        DOWN: ("owners", feature_rows(wd_ref), unit_columns(down), True),
+        UP: ("owners", feature_columns(wu_ref), unit_rows(up), True),
+        PRE: ("owners", by_rank(pre_out), by_step(pre_in), False),
+        UPS: ("owners", by_rank(ups_out), by_step(ups_in), False),
+        ACT: ("owners", mine(act), mine(act), False),
+        DPRE: ("owners", mine(dpre), mine(dpre), False),
+        OUT: ("across", group_rows(out), group_rows(out_ref), True),
+        BACK: ("across", group_rows(back), group_rows(back_ref), True),
+        GUP: ("owners", by_rank(gup), feature_columns(gu_ref), True),
+        GDOWN: ("owners", by_rank(gdown), feature_rows(gd_ref), True),
+    }
+
+    def remote(name, step):
+        kind, take, put, _ = moves[name]
+        peer = peer_of(kind, me, step, devices)
+        return pltpu.make_async_remote_copy(
+            src_ref=take(peer, step),
+            dst_ref=put(me, step),
+            send_sem=send.at[name, step],
+            recv_sem=recv.at[name, step],
+            device_id={"fsdp": peer},
+            device_id_type=pl.DeviceIdType.MESH,
+        )
+
+    def local(name):
+        _, take, put, _ = moves[name]
+        return pltpu.make_async_copy(take(me, 0), put(me, 0), own.at[name])
+
+    def begin(name):
+        def body(step, carry):
+            remote(name, step).start()
+            return carry
+
+        lax.fori_loop(1, size_of(moves[name][0], devices), body, 0)
+        if moves[name][3]:
+            local(name).start()
+
+    def finish(name):
+        def body(step, carry):
+            remote(name, step).wait()
+            return carry
+
+        lax.fori_loop(1, size_of(moves[name][0], devices), body, 0)
+        if moves[name][3]:
+            local(name).wait()
+
+    def dot(left, right, over):
+        return lax.dot_general(left, right, ((over[:1], over[1:]), ((), ())), preferred_element_type=f32)
+
+    def each(count, body):
+        def wrapped(index, carry):
+            body(index)
+            return carry
+
+        lax.fori_loop(0, count, wrapped, 0)
+
+    def gathered(ref, at):
+        return jnp.concatenate([ref[owner, at, :] for owner in range(OWN)], axis=1)
+
+    begin(TOK)
+    begin(DOWN)
+    finish(TOK)
+    finish(DOWN)
+    begin(COT)
+    begin(UP)
+
+    def pre_tile(index):
+        at = span(index, ROW_TILE)
+        block = rows[at, :]
+        for owner in range(OWN):
+            columns = pl.ds(owner * units, units)
+            pre_out[owner, at, :] = dot(block, down[:, columns], (1, 0)).astype(bf16)
+
+    each(tiles, pre_tile)
+    begin(PRE)
+    finish(PRE)
+
+    def act_tile(index):
+        at = span(index, ROW_TILE)
+        value = pre_out[rank, at, :].astype(f32)
+        for step in range(OWN - 1):
+            value = value + pre_in[step, at, :].astype(f32)
+        square = value * value
+        bent = jnp.tanh(GELU_C * (value + 0.044715 * (square * value)))
+        half = 0.5 * (1.0 + bent)
+        act[rank, at, :] = (value * half).astype(bf16)
+        slope[at, :] = half + (0.5 * GELU_C) * value * (1.0 - bent * bent) * (
+            1.0 + (3.0 * 0.044715) * square
+        )
+
+    each(tiles, act_tile)
+    begin(ACT)
+    finish(COT)
+    finish(UP)
+
+    def ups_tile(index):
+        at = span(index, ROW_TILE)
+        block = cots[at, :]
+        for owner in range(OWN):
+            ups_out[owner, at, :] = dot(block, up[pl.ds(owner * units, units), :], (1, 1)).astype(
+                bf16
+            )
+
+    each(tiles, ups_tile)
+    finish(ACT)
+    begin(UPS)
+
+    def out_tile(index):
+        at = span(index, ROW_TILE)
+        block = gathered(act, at)
+        for first in range(0, quarter, wide):
+            columns = pl.ds(first, wide)
+            out[at, columns] = dot(block, up[:, columns], (1, 0)).astype(bf16)
+
+    each(tiles, out_tile)
+    begin(OUT)
+    finish(UPS)
+
+    def dpre_tile(index):
+        at = span(index, ROW_TILE)
+        value = ups_out[rank, at, :].astype(f32)
+        for step in range(OWN - 1):
+            value = value + ups_in[step, at, :].astype(f32)
+        dpre[rank, at, :] = (slope[at, :] * value).astype(bf16)
+
+    each(tiles, dpre_tile)
+    begin(DPRE)
+
+    def gup_tile(owner):
+        left = act[owner]
+        for first in range(0, quarter, wide):
+            columns = pl.ds(first, wide)
+            gup[owner, :, columns] = (dot(left, cots[:, columns], (0, 0)) * grad_scale).astype(bf16)
+
+    each(OWN, gup_tile)
+    finish(DPRE)
+    begin(GUP)
+
+    def back_tile(index):
+        at = span(index, ROW_TILE)
+        block = gathered(dpre, at)
+        for first in range(0, quarter, wide):
+            columns = pl.ds(first, wide)
+            back[at, columns] = dot(block, down[columns, :], (1, 1)).astype(bf16)
+
+    each(tiles, back_tile)
+    begin(BACK)
+
+    def gdown_tile(owner):
+        right = dpre[owner]
+        for first in range(0, quarter, wide):
+            columns = pl.ds(first, wide)
+            gdown[owner, columns, :] = (dot(rows[:, columns], right, (0, 0)) * grad_scale).astype(
+                bf16
+            )
+
+    each(OWN, gdown_tile)
+    begin(GDOWN)
+    for name in (GUP, OUT, GDOWN, BACK):
+        finish(name)
+
+
+def adapter(devices, grad_scale, tok, cot, w_down, w_up):
+    bf16 = jnp.bfloat16
+    slots, quarter = tok.shape
+    width, units = w_down.shape
+    hidden = units * OWN
+    steps = max(devices // OWN, OWN)
+    whole = pltpu.VMEM((OWN, slots, units), bf16)
+    received = pltpu.VMEM((OWN - 1, slots, units), bf16)
+    wide_rows = pltpu.VMEM((slots, quarter), bf16)
+    return pl.pallas_call(
+        functools.partial(adapter_kernel, devices, grad_scale),
+        out_shape=[
+            jax.ShapeDtypeStruct((slots, quarter), bf16),
+            jax.ShapeDtypeStruct((slots, quarter), bf16),
+            jax.ShapeDtypeStruct((width, units), bf16),
+            jax.ShapeDtypeStruct((units, width), bf16),
+        ],
+        in_specs=[ANY] * 4,
+        out_specs=[ANY] * 4,
+        scratch_shapes=[
+            wide_rows,
+            wide_rows,
+            pltpu.VMEM((quarter, hidden), bf16),
+            pltpu.VMEM((hidden, quarter), bf16),
+            whole,
+            received,
+            whole,
+            received,
+            whole,
+            whole,
+            pltpu.VMEM((slots, units), jnp.float32),
+            wide_rows,
+            wide_rows,
+            pltpu.VMEM((OWN, units, quarter), bf16),
+            pltpu.VMEM((OWN, quarter, units), bf16),
+            pltpu.SemaphoreType.DMA((TRANSFERS, steps)),
+            pltpu.SemaphoreType.DMA((TRANSFERS, steps)),
+            pltpu.SemaphoreType.DMA((TRANSFERS,)),
+        ],
+        compiler_params=pltpu.CompilerParams(
+            collective_id=2, has_side_effects=True, vmem_limit_bytes=48 * 1024 * 1024
+        ),
+    )(tok, cot, w_down, w_up)
+
+
 def per_device(tokens, cotangent, block_lang, gain, w_down, w_up):
     bf16, f32 = jnp.bfloat16, jnp.float32
     devices = lax.axis_size("fsdp")
@@ -199,110 +469,21 @@
     def pick(values):
         return jnp.where(filled[:, :, None, None], values[table], jnp.zeros((), bf16))
 
-    def at_place(ref, me):
-        return ref.at[me // OWN]
-
-    rows_in, cot_in, down, up = exchange(
-        devices,
-        2,
-        [
-            ("across", [(0, piece, 0, at_place), (1, piece, 1, at_place)]),
-            (
-                "owners",
-                [
-                    (
-                        2,
-                        lambda ref, peer: ref.at[span(lax.rem(peer, OWN), quarter), :],
-                        2,
-                        lambda ref, me: ref.at[:, span(lax.rem(me, OWN), units)],
-                    ),
-                    (
-                        3,
-                        lambda ref, peer: ref.at[:, span(lax.rem(peer, OWN), quarter)],
-                        3,
-                        lambda ref, me: ref.at[span(lax.rem(me, OWN), units), :],
-                    ),
-                ],
-            ),
-        ],
-        [pick(normed), pick(spread_cot), w_down, w_up],
-        [
-            ((languages, MOSTB, rows, quarter), bf16),
-            ((languages, MOSTB, rows, quarter), bf16),
-            ((quarter, hidden), bf16),
-            ((hidden, quarter), bf16),
-        ],
-    )
-    rows_in = rows_in.reshape(slots, quarter)
-    cot_in = cot_in.reshape(slots, quarter)
-
-    part_pre = jnp.dot(rows_in, down, preferred_element_type=f32).astype(bf16)
-    part_up = jnp.dot(cot_in, up.T, preferred_element_type=f32).astype(bf16)
-
-    def unit_span(ref, peer):
-        return ref.at[:, span(lax.rem(peer, OWN), units)]
-
-    def at_rank(ref, me):
-        return ref.at[lax.rem(me, OWN)]
-
-    pre_parts, up_parts = exchange(
-        devices,
-        3,
-        [("owners", [(0, unit_span, 0, at_rank), (1, unit_span, 1, at_rank)])],
-        [part_pre, part_up],
-        [((OWN, slots, units), bf16), ((OWN, slots, units), bf16)],
-    )
-    preact = jnp.sum(pre_parts, axis=0, dtype=f32)
-    upstream = jnp.sum(up_parts, axis=0, dtype=f32)
-    activ_wide, pullback = jax.vjp(gelu_tanh, preact)
-    dpreact_here = pullback(upstream)[0].astype(bf16)
-
-    def all_of(ref, peer):
-        return ref
-
-    activation, dpreact = exchange(
-        devices,
-        4,
-        [("owners", [(0, all_of, 0, unit_span), (1, all_of, 1, unit_span)])],
-        [activ_wide.astype(bf16), dpreact_here],
-        [((slots, hidden), bf16), ((slots, hidden), bf16)],
-    )
-    shape = (languages, MOSTB, rows, quarter)
-    out = jnp.dot(activation, up, preferred_element_type=f32).astype(bf16).reshape(shape)
-    back = jnp.dot(dpreact, down.T, preferred_element_type=f32).astype(bf16).reshape(shape)
-    part_grad_up = (
-        jnp.dot(activation.T, cot_in, preferred_element_type=f32) * grad_scale
-    ).astype(bf16)
-    part_grad_down = (
-        jnp.dot(rows_in.T, dpreact, preferred_element_type=f32) * grad_scale
-    ).astype(bf16)
-
-    out_home, back_home, grad_down, grad_up = exchange(
-        devices,
-        5,
-        [
-            ("across", [(0, piece, 0, at_place), (1, piece, 1, at_place)]),
-            (
-                "owners",
-                [
-                    (
-                        2,
-                        unit_span,
-                        2,
-                        lambda ref, me: ref.at[span(lax.rem(me, OWN), quarter), :],
-                    ),
-                    (
-                        3,
-                        lambda ref, peer: ref.at[span(lax.rem(peer, OWN), units), :],
-                        3,
-                        lambda ref, me: ref.at[:, span(lax.rem(me, OWN), quarter)],
-                    ),
-                ],
-            ),
-        ],
-        [out, back, part_grad_down, part_grad_up],
-        [(shape, bf16), (shape, bf16), ((width, units), bf16), ((units, width), bf16)],
-    )
+    chunk = -(-MOSTB * rows // 16) * 16
+
+    def packed(values):
+        picked = pick(values).reshape(languages, MOSTB * rows, quarter)
+        filler = ((0, 0), (0, chunk - MOSTB * rows), (0, 0))
+        return jnp.pad(picked, filler).reshape(languages * chunk, quarter)
+
+    def unpacked(values):
+        shaped = values.reshape(languages, chunk, quarter)[:, : MOSTB * rows]
+        return shaped.reshape(languages, MOSTB, rows, quarter)
+
+    out_home, back_home, grad_down, grad_up = adapter(
+        devices, grad_scale, packed(normed), packed(spread_cot), w_down, w_up
+    )
+    out_home, back_home = unpacked(out_home), unpacked(back_home)
     branch_rows = out_home[block_lang, ranks]
     dnormed_rows = back_home[block_lang, ranks]
     gain_part = jnp.sum(dnormed_rows.astype(f32) * unit_rows, axis=(0, 1))
@@ -312,7 +493,7 @@
 
     branch, dnormed, gain_parts = exchange(
         devices,
-        6,
+        3,
         [
             (
                 "all",

time: 387 us -> 321 us (0.83)
  Pallas kernels: 328 us -> 290 us
  matrix products: 22.1 us -> 0 us
    pallas_call x6 -> x2, Pallas kernels: 328 us -> 114 us  [exchange(): pl.pallas_call(functools.partial(exchange_kernel, devices, plans, len(inp...]
    pallas_call x0 -> x1, Pallas kernels: none -> 176 us  [adapter(): pl.pallas_call(functools.partial(adapter_kernel, devices, grad_scale), ou...]
    dot_general x6 -> x0, matrix products: 22.1 us -> none  [the longest x1 5.18 us: per_device(): part_up = jnp.dot(cot_in, up.T, preferred_element_type=f32).astype(bf16)]
where the time goes in v2:
time: 321 us
  Pallas kernels  290 us (90%)
  local copies, waits for them, and re-layouts  15.1 us (5%)
  other arithmetic  14.5 us (5%)
    pallas_call x1, Pallas kernels, adapter(): pl.pallas_call(functools.partial(adapter_kernel, devices, grad_scale), ou...  176 us
    pallas_call x2, Pallas kernels, exchange(): pl.pallas_call(functools.partial(exchange_kernel, devices, plans, len(inp...  114 us

profile of v2, /device:TPU:13, one launch (start us, length us, event | category | flops | bytes accessed | tf_op | source)
XLA Modules:
  0.0 320.6 jit_solution(11826502256827413970)
XLA Ops:
  0.7 1.5 fusion
  2.3 0.7 fusion.7
  3.1 0.8 fusion.8
  4.0 0.7 fusion.16
  5.3 1.3 broadcast_in_dim.60.refs_3_
  6.5 0.7 broadcast_in_dim.33.refs_2_
  7.3 60.0 %shard_map.101 = (bf16[16,32,1024]{2,1,0:T(8,128)(2,1)}, bf16[16,32,1024]{2,1,0:T(8,128)(2,1)}, f32[16,32,128]{2,1,0:T(8,128)}, f32[16,8,256]{2,1,0:T(8,128)}) custom-call(bf16[4,32,4096]{2,1,0:T(8,128)(2,1)} %bitcast.37, bf16[4,32,4096]{2,1,0:T(8,128)(2,1)} %bitcast.40, f32[4,32,128]{2,1,0:T(8,128)} %broadcast_in_dim.33.refs_2_, ...), custom_call_target="tpu_custom_call" | custom-call | tf_op jit(solution)/shard_map/pallas_call | solution.py:119
  67.2 1.1 slice_reduce_fusion
  68.3 0.9 slice.10
  69.3 1.6 multiply_convert_fusion
  70.9 0.6 gather_fusion
  71.6 1.9 gather_fusion.1
  73.4 1.7 bitcast_select_fusion
  75.2 176.3 %shard_map.102 = (bf16[768,1024]{1,0:T(8,128)(2,1)S(1)}, bf16[768,1024]{1,0:T(8,128)(2,1)S(1)}, bf16[4096,256]{1,0:T(8,128)(2,1)}, bf16[256,4096]{1,0:T(8,128)(2,1)}) custom-call(bf16[768,1024]{1,0:T(8,128)(2,1)S(1)} %get-tuple-element.32.tok_ref, bf16[768,1024]{1,0:T(8,128)(2,1)} %get-tuple-element.31.cot_ref, bf16[4096,256]{1,0:T(8,128)(2,1)} %wd_ref.1, ...), custom_call_target="tpu_custom_call" | custom-call | tf_op jit(solution)/shard_map/pallas_call | solution.py:369
  251.5 1.6 gather_fusion.2
  253.7 2.2 multiply_reduce_fusion.1
  255.9 0.6 broadcast_in_dim.64.refs_2_
  256.5 53.9 %shard_map.103 = (bf16[4,32,4096]{2,1,0:T(8,128)(2,1)}, bf16[4,32,4096]{2,1,0:T(8,128)(2,1)}, f32[16,8,256]{2,1,0:T(8,128)}) custom-call(bf16[16,32,1024]{2,1,0:T(8,128)(2,1)} %gather_fusion.2, bf16[16,32,1024]{2,1,0:T(8,128)(2,1)} %copy-done.1, f32[4,8,256]{2,1,0:T(8,128)} %broadcast_in_dim.64.refs_2_), custom_call_target="tpu_custom_call" | custom-call | tf_op jit(solution)/shard_map/pallas_call | solution.py:119
  310.4 1.9 multiply_reduce_fusion
  312.4 1.0 slice_reduce_fusion.1
  314.7 2.2 fusion.6
  316.9 1.3 copy.16
  318.2 1.0 copy-done.4
  319.3 1.3 copy.17
  (35 shorter events, 2.8 us)
Async XLA Ops:
  253.7 2.8 copy-start.1
  253.7 56.7 %copy-start = (bf16[1,128,4096]{2,1,0:T(8,128)(2,1)S(1)}, bf16[1,128,4096]{2,1,0:T(8,128)(2,1)}, u32[]{:S(2)}) copy-start(bf16[1,128,4096]{2,1,0:T(8,128)(2,1)} %param.6) | copy-start | bytes 3145732
  310.4 3.6 %copy-start.2 = (bf16[4,32,4096]{2,1,0:T(8,128)(2,1)S(1)}, bf16[4,32,4096]{2,1,0:T(8,128)(2,1)}, u32[]{:S(2)}) copy-start(bf16[4,32,4096]{2,1,0:T(8,128)(2,1)} %get-tuple-element.23) | copy-start | bytes 3145732
  312.3 2.0 copy-start.3
  313.4 1.3 copy-start.6
  314.7 2.2 copy-start.5
  316.9 2.3 copy-start.4

commit v3 on v2

--- a/solution.py
+++ b/solution.py
@@ -149,7 +149,9 @@
     languages = devices // OWN
     slots, quarter = rows.shape
     chunk = slots // languages
-    units = wd_ref.shape[1]
+    units = wu_ref.shape[0]
+    side, core = rank // 2, lax.rem(rank, 2)
+    twin, facing, opposite = side * 2 + 1 - core, (1 - side) * 2 + core, (1 - side) * 2 + 1 - core
     wide = min(512, quarter)
     tiles = slots // ROW_TILE
 
@@ -180,27 +182,13 @@
     def unit_rows(ref):
         return lambda device, step: ref.at[span(lax.rem(device, OWN), units), :]
 
-    def unit_columns(ref):
-        return lambda device, step: ref.at[:, span(lax.rem(device, OWN), units)]
-
     def by_rank(ref):
         return lambda device, step: ref.at[lax.rem(device, OWN)]
-
-    def by_step(ref):
-        return lambda device, step: ref.at[step - 1]
-
-    def mine(ref):
-        return lambda device, step: ref.at[rank]
 
     moves = {
         TOK: ("across", group_rows(tok_ref), group_rows(rows), True),
         COT: ("across", group_rows(cot_ref), group_rows(cots), True),
-        DOWN: ("owners", feature_rows(wd_ref), unit_columns(down), True),
         UP: ("owners", feature_columns(wu_ref), unit_rows(up), True),
-        PRE: ("owners", by_rank(pre_out), by_step(pre_in), False),
-        UPS: ("owners", by_rank(ups_out), by_step(ups_in), False),
-        ACT: ("owners", mine(act), mine(act), False),
-        DPRE: ("owners", mine(dpre), mine(dpre), False),
         OUT: ("across", group_rows(out), group_rows(out_ref), True),
         BACK: ("across", group_rows(back), group_rows(back_ref), True),
         GUP: ("owners", by_rank(gup), feature_columns(gu_ref), True),
@@ -241,6 +229,53 @@
         if moves[name][3]:
             local(name).wait()
 
+    def direct(name, slot, source, target, rank_to):
+        return pltpu.make_async_remote_copy(
+            src_ref=source,
+            dst_ref=target,
+            send_sem=send.at[name, slot],
+            recv_sem=recv.at[name, slot],
+            device_id={"fsdp": group * OWN + rank_to},
+            device_id_type=pl.DeviceIdType.MESH,
+        )
+
+    def reduce(name, parts, landed, beside=None):
+        final = direct(name, 1, parts.at[twin], landed.at[0], twin)
+        paired = direct(name, 2, parts.at[opposite], landed.at[1], twin)
+        paired.start()
+        final.start()
+        paired.wait()
+
+        def pair_tile(index):
+            at = span(index, ROW_TILE)
+            both = parts[facing, at, :].astype(f32) + landed[1, at, :].astype(f32)
+            parts[facing, at, :] = both.astype(bf16)
+
+        each(tiles, pair_tile)
+        crossing = direct(name, 3, parts.at[facing], landed.at[2], facing)
+        crossing.start()
+        if beside is not None:
+            beside()
+        final.wait()
+        crossing.wait()
+
+    def reduced(parts, landed, at):
+        value = parts[rank, at, :].astype(f32) + landed[0, at, :].astype(f32)
+        return value + landed[2, at, :].astype(f32)
+
+    def gather(name, ref, beside=None):
+        across = direct(name, 2, ref.at[rank], ref.at[rank], facing)
+        beside_me = direct(name, 1, ref.at[rank], ref.at[rank], twin)
+        across.start()
+        beside_me.start()
+        if beside is not None:
+            beside()
+        across.wait()
+        passed = direct(name, 3, ref.at[facing], ref.at[facing], twin)
+        passed.start()
+        beside_me.wait()
+        passed.wait()
+
     def dot(left, right, over):
         return lax.dot_general(left, right, ((over[:1], over[1:]), ((), ())), preferred_element_type=f32)
 
@@ -255,11 +290,12 @@
         return jnp.concatenate([ref[owner, at, :] for owner in range(OWN)], axis=1)
 
     begin(TOK)
-    begin(DOWN)
+    begin(UP)
+    load_down = pltpu.make_async_copy(wd_ref, down, own.at[DOWN])
+    load_down.start()
+    load_down.wait()
     finish(TOK)
-    finish(DOWN)
     begin(COT)
-    begin(UP)
 
     def pre_tile(index):
         at = span(index, ROW_TILE)
@@ -269,14 +305,11 @@
             pre_out[owner, at, :] = dot(block, down[:, columns], (1, 0)).astype(bf16)
 
     each(tiles, pre_tile)
-    begin(PRE)
-    finish(PRE)
+    reduce(PRE, pre_out, pre_in)
 
     def act_tile(index):
         at = span(index, ROW_TILE)
-        value = pre_out[rank, at, :].astype(f32)
-        for step in range(OWN - 1):
-            value = value + pre_in[step, at, :].astype(f32)
+        value = reduced(pre_out, pre_in, at)
         square = value * value
         bent = jnp.tanh(GELU_C * (value + 0.044715 * (square * value)))
         half = 0.5 * (1.0 + bent)
@@ -286,9 +319,19 @@
         )
 
     each(tiles, act_tile)
-    begin(ACT)
+    gather(ACT, act)
+    finish(UP)
+
+    def out_tile(index):
+        at = span(index, ROW_TILE)
+        block = gathered(act, at)
+        for first in range(0, quarter, wide):
+            columns = pl.ds(first, wide)
+            out[at, columns] = dot(block, up[:, columns], (1, 0)).astype(bf16)
+
+    each(tiles, out_tile)
+    begin(OUT)
     finish(COT)
-    finish(UP)
 
     def ups_tile(index):
         at = span(index, ROW_TILE)
@@ -299,29 +342,6 @@
             )
 
     each(tiles, ups_tile)
-    finish(ACT)
-    begin(UPS)
-
-    def out_tile(index):
-        at = span(index, ROW_TILE)
-        block = gathered(act, at)
-        for first in range(0, quarter, wide):
-            columns = pl.ds(first, wide)
-            out[at, columns] = dot(block, up[:, columns], (1, 0)).astype(bf16)
-
-    each(tiles, out_tile)
-    begin(OUT)
-    finish(UPS)
-
-    def dpre_tile(index):
-        at = span(index, ROW_TILE)
-        value = ups_out[rank, at, :].astype(f32)
-        for step in range(OWN - 1):
-            value = value + ups_in[step, at, :].astype(f32)
-        dpre[rank, at, :] = (slope[at, :] * value).astype(bf16)
-
-    each(tiles, dpre_tile)
-    begin(DPRE)
 
     def gup_tile(owner):
         left = act[owner]
@@ -329,8 +349,15 @@
             columns = pl.ds(first, wide)
             gup[owner, :, columns] = (dot(left, cots[:, columns], (0, 0)) * grad_scale).astype(bf16)
 
-    each(OWN, gup_tile)
-    finish(DPRE)
+    reduce(UPS, ups_out, ups_in, lambda: each(OWN, gup_tile))
+
+    def dpre_tile(index):
+        at = span(index, ROW_TILE)
+        value = reduced(ups_out, ups_in, at)
+        dpre[rank, at, :] = (slope[at, :] * value).astype(bf16)
+
+    each(tiles, dpre_tile)
+    gather(DPRE, dpre)
     begin(GUP)
 
     def back_tile(index):
@@ -357,10 +384,10 @@
         finish(name)
 
 
-def adapter(devices, grad_scale, tok, cot, w_down, w_up):
+def adapter(devices, grad_scale, tok, cot, down, w_up):
     bf16 = jnp.bfloat16
     slots, quarter = tok.shape
-    width, units = w_down.shape
+    units, width = w_up.shape
     hidden = units * OWN
     steps = max(devices // OWN, OWN)
     whole = pltpu.VMEM((OWN, slots, units), bf16)
@@ -399,7 +426,7 @@
         compiler_params=pltpu.CompilerParams(
             collective_id=2, has_side_effects=True, vmem_limit_bytes=48 * 1024 * 1024
         ),
-    )(tok, cot, w_down, w_up)
+    )(tok, cot, down, w_up)
 
 
 def per_device(tokens, cotangent, block_lang, gain, w_down, w_up):
@@ -434,7 +461,7 @@
     def at_device(ref, me):
         return ref.at[me]
 
-    spread_tok, spread_cot, spread_root, gain_all = exchange(
+    spread_tok, spread_cot, spread_root, gain_all, down = exchange(
         devices,
         1,
         [
@@ -446,19 +473,32 @@
                     (0, slab, 0, at_device),
                     (1, slab, 1, at_device),
                 ],
-            )
+            ),
+            (
+                "owners",
+                [
+                    (
+                        4,
+                        lambda ref, peer: ref.at[span(lax.rem(peer, OWN), quarter), :],
+                        4,
+                        lambda ref, me: ref.at[:, span(lax.rem(me, OWN), units)],
+                    )
+                ],
+            ),
         ],
         [
             tokens.reshape(languages, rows, width),
             cotangent.reshape(languages, rows, width),
             jnp.broadcast_to(root_mean, (per_block, 128)).reshape(languages, rows, 128),
             jnp.broadcast_to(gain, (1, 8, gain_width)),
+            w_down,
         ],
         [
             ((devices, rows, quarter), bf16),
             ((devices, rows, quarter), bf16),
             ((devices, rows, 128), f32),
             ((devices, 8, gain_width), f32),
+            ((quarter, units * OWN), bf16),
         ],
     )
     gain_full = gain_all[:, 0, :].reshape(width)
@@ -481,7 +521,7 @@
         return shaped.reshape(languages, MOSTB, rows, quarter)
 
     out_home, back_home, grad_down, grad_up = adapter(
-        devices, grad_scale, packed(normed), packed(spread_cot), w_down, w_up
+        devices, grad_scale, packed(normed), packed(spread_cot), down, w_up
     )
     out_home, back_home = unpacked(out_home), unpacked(back_home)
     branch_rows = out_home[block_lang, ranks]

time: 321 us -> 305 us (0.950)
  Pallas kernels: 290 us -> 274 us
    pallas_call x1, Pallas kernels: 176 us -> 160 us  [adapter(): pl.pallas_call(functools.partial(adapter_kernel, devices, grad_scale), ou...]
where the time goes in v3:
time: 305 us
  Pallas kernels  274 us (90%)
  local copies, waits for them, and re-layouts  15.1 us (5%)
  other arithmetic  14.5 us (5%)
    pallas_call x1, Pallas kernels, adapter(): pl.pallas_call(functools.partial(adapter_kernel, devices, grad_scale), ou...  160 us
    pallas_call x2, Pallas kernels, exchange(): pl.pallas_call(functools.partial(exchange_kernel, devices, plans, len(inp...  114 us

profile of v3, /device:TPU:13, one launch (start us, length us, event | category | flops | bytes accessed | tf_op | source)
XLA Modules:
  0.0 304.7 jit_solution(11083794277828554284)
XLA Ops:
  0.7 1.5 fusion
  2.3 0.7 fusion.7
  3.1 0.8 fusion.8
  4.0 0.7 fusion.16
  5.3 1.3 broadcast_in_dim.60.refs_3_
  6.5 0.7 broadcast_in_dim.33.refs_2_
  7.3 60.1 %shard_map.101 = (bf16[16,32,1024]{2,1,0:T(8,128)(2,1)}, bf16[16,32,1024]{2,1,0:T(8,128)(2,1)}, f32[16,32,128]{2,1,0:T(8,128)}, f32[16,8,256]{2,1,0:T(8,128)}, bf16[1024,1024]{1,0:T(8,128)(2,1)}) custom-call(bf16[4,32,4096]{2,1,0:T(8,128)(2,1)} %bitcast.37, bf16[4,32,4096]{2,1,0:T(8,128)(2,1)} %bitcast.40, f32[4,32,128]{2,1,0:T(8,128)} %broadcast_in_dim.33.refs_2_, ...), custom_call_target="tpu_custom_call" | custom-call | tf_op jit(solution)/shard_map/pallas_call | solution.py:119
  67.4 1.1 slice_reduce_fusion
  68.5 0.9 slice.10
  69.4 1.6 multiply_convert_fusion
  71.1 0.6 gather_fusion
  71.7 1.9 gather_fusion.1
  73.6 1.7 bitcast_select_fusion
  75.4 159.9 %shard_map.102 = (bf16[768,1024]{1,0:T(8,128)(2,1)S(1)}, bf16[768,1024]{1,0:T(8,128)(2,1)S(1)}, bf16[4096,256]{1,0:T(8,128)(2,1)}, bf16[256,4096]{1,0:T(8,128)(2,1)}) custom-call(bf16[768,1024]{1,0:T(8,128)(2,1)S(1)} %get-tuple-element.34.tok_ref, bf16[768,1024]{1,0:T(8,128)(2,1)} %get-tuple-element.33.cot_ref, bf16[1024,1024]{1,0:T(8,128)(2,1)} %get-tuple-element.21.wd_ref, ...), custom_call_target="tpu_custom_call" | custom-call | tf_op jit(solution)/shard_map/pallas_call | solution.py:396
  235.3 1.6 gather_fusion.2
  237.5 2.2 multiply_reduce_fusion.1
  239.7 0.6 broadcast_in_dim.64.refs_2_
  240.3 54.2 %shard_map.103 = (bf16[4,32,4096]{2,1,0:T(8,128)(2,1)}, bf16[4,32,4096]{2,1,0:T(8,128)(2,1)}, f32[16,8,256]{2,1,0:T(8,128)}) custom-call(bf16[16,32,1024]{2,1,0:T(8,128)(2,1)} %gather_fusion.2, bf16[16,32,1024]{2,1,0:T(8,128)(2,1)} %copy-done.1, f32[4,8,256]{2,1,0:T(8,128)} %broadcast_in_dim.64.refs_2_), custom_call_target="tpu_custom_call" | custom-call | tf_op jit(solution)/shard_map/pallas_call | solution.py:119
  294.5 1.9 multiply_reduce_fusion
  296.5 1.0 slice_reduce_fusion.1
  298.8 2.2 fusion.6
  301.0 1.3 copy.16
  302.4 1.0 copy-done.4
  303.4 1.3 copy.17
  (35 shorter events, 2.8 us)
Async XLA Ops:
  237.5 2.8 copy-start.1
  237.5 57.0 %copy-start = (bf16[1,128,4096]{2,1,0:T(8,128)(2,1)S(1)}, bf16[1,128,4096]{2,1,0:T(8,128)(2,1)}, u32[]{:S(2)}) copy-start(bf16[1,128,4096]{2,1,0:T(8,128)(2,1)} %param.6) | copy-start | bytes 3145732
  294.5 3.6 %copy-start.2 = (bf16[4,32,4096]{2,1,0:T(8,128)(2,1)S(1)}, bf16[4,32,4096]{2,1,0:T(8,128)(2,1)}, u32[]{:S(2)}) copy-start(bf16[4,32,4096]{2,1,0:T(8,128)(2,1)} %get-tuple-element.25) | copy-start | bytes 3145732
  296.4 2.0 copy-start.3
  297.5 1.3 copy-start.6
  298.8 2.2 copy-start.5
  301.0 2.3 copy-start.4

commit v4 on v3

--- a/solution.py
+++ b/solution.py
@@ -173,9 +173,6 @@
     def group_rows(ref):
         return lambda device, step: ref.at[span(device // OWN, chunk), :]
 
-    def feature_rows(ref):
-        return lambda device, step: ref.at[span(lax.rem(device, OWN), quarter), :]
-
     def feature_columns(ref):
         return lambda device, step: ref.at[:, span(lax.rem(device, OWN), quarter)]
 
@@ -192,7 +189,6 @@
         OUT: ("across", group_rows(out), group_rows(out_ref), True),
         BACK: ("across", group_rows(back), group_rows(back_ref), True),
         GUP: ("owners", by_rank(gup), feature_columns(gu_ref), True),
-        GDOWN: ("owners", by_rank(gdown), feature_rows(gd_ref), True),
     }
 
     def remote(name, step):
@@ -379,9 +375,11 @@
             )
 
     each(OWN, gdown_tile)
-    begin(GDOWN)
-    for name in (GUP, OUT, GDOWN, BACK):
+    store_gdown = pltpu.make_async_copy(gdown, gd_ref, own.at[GDOWN])
+    store_gdown.start()
+    for name in (GUP, OUT, BACK):
         finish(name)
+    store_gdown.wait()
 
 
 def adapter(devices, grad_scale, tok, cot, down, w_up):
@@ -398,7 +396,7 @@
         out_shape=[
             jax.ShapeDtypeStruct((slots, quarter), bf16),
             jax.ShapeDtypeStruct((slots, quarter), bf16),
-            jax.ShapeDtypeStruct((width, units), bf16),
+            jax.ShapeDtypeStruct((OWN, quarter, units), bf16),
             jax.ShapeDtypeStruct((units, width), bf16),
         ],
         in_specs=[ANY] * 4,
@@ -520,7 +518,7 @@
         shaped = values.reshape(languages, chunk, quarter)[:, : MOSTB * rows]
         return shaped.reshape(languages, MOSTB, rows, quarter)
 
-    out_home, back_home, grad_down, grad_up = adapter(
+    out_home, back_home, part_grad_down, grad_up = adapter(
         devices, grad_scale, packed(normed), packed(spread_cot), down, w_up
     )
     out_home, back_home = unpacked(out_home), unpacked(back_home)
@@ -531,7 +529,7 @@
     def at_home(ref, me):
         return ref.at[me // OWN, :, span(lax.rem(me, OWN), quarter)]
 
-    branch, dnormed, gain_parts = exchange(
+    branch, dnormed, gain_parts, grad_down = exchange(
         devices,
         3,
         [
@@ -542,7 +540,18 @@
                     (0, at_device, 0, at_home),
                     (1, at_device, 1, at_home),
                 ],
-            )
+            ),
+            (
+                "owners",
+                [
+                    (
+                        3,
+                        lambda ref, peer: ref.at[lax.rem(peer, OWN)],
+                        3,
+                        lambda ref, me: ref.at[span(lax.rem(me, OWN), quarter), :],
+                    )
+                ],
+            ),
         ],
         [
             branch_rows,
@@ -550,11 +559,13 @@
             jnp.broadcast_to(
                 gain_part.reshape(languages, 1, gain_width), (languages, 8, gain_width)
             ),
+            part_grad_down,
         ],
         [
             ((languages, rows, width), bf16),
             ((languages, rows, width), bf16),
             ((devices, 8, gain_width), f32),
+            ((width, units), bf16),
         ],
     )
     holders = gain_parts[:, 0, :].reshape(languages, OWN, gain_width)

time: 305 us -> 289 us (0.948)
  Pallas kernels: 274 us -> 257 us
    pallas_call x1, Pallas kernels: 160 us -> 138 us  [adapter(): pl.pallas_call(functools.partial(adapter_kernel, devices, grad_scale), ou...]
    pallas_call x2, Pallas kernels: 114 us -> 119 us  [exchange(): pl.pallas_call(functools.partial(exchange_kernel, devices, plans, len(inp...]
where the time goes in v4:
time: 289 us; the launch traced here: 287 us
  Pallas kernels  257 us (89%)
  local copies, waits for them, and re-layouts  15.1 us (5%)
  other arithmetic  14.5 us (5%)
    pallas_call x1, Pallas kernels, adapter(): pl.pallas_call(functools.partial(adapter_kernel, devices, grad_scale), ou...  138 us
    pallas_call x2, Pallas kernels, exchange(): pl.pallas_call(functools.partial(exchange_kernel, devices, plans, len(inp...  119 us

profile of v4, /device:TPU:13, one launch (start us, length us, event | category | flops | bytes accessed | tf_op | source)
XLA Modules:
  0.0 287.3 jit_solution(13398651407781613310)
XLA Ops:
  0.7 1.5 fusion
  2.3 0.7 fusion.7
  3.1 0.8 fusion.8
  4.0 0.7 fusion.16
  5.3 1.3 broadcast_in_dim.60.refs_3_
  6.5 0.7 broadcast_in_dim.33.refs_2_
  7.3 60.1 %shard_map.101 = (bf16[16,32,1024]{2,1,0:T(8,128)(2,1)}, bf16[16,32,1024]{2,1,0:T(8,128)(2,1)}, f32[16,32,128]{2,1,0:T(8,128)}, f32[16,8,256]{2,1,0:T(8,128)}, bf16[1024,1024]{1,0:T(8,128)(2,1)}) custom-call(bf16[4,32,4096]{2,1,0:T(8,128)(2,1)} %bitcast.37, bf16[4,32,4096]{2,1,0:T(8,128)(2,1)} %bitcast.40, f32[4,32,128]{2,1,0:T(8,128)} %broadcast_in_dim.33.refs_2_, ...), custom_call_target="tpu_custom_call" | custom-call | tf_op jit(solution)/shard_map/pallas_call | solution.py:119
  67.4 1.1 slice_reduce_fusion
  68.5 0.9 slice.10
  69.4 1.6 multiply_convert_fusion
  71.1 0.6 gather_fusion
  71.7 1.9 gather_fusion.1
  73.6 1.7 bitcast_select_fusion
  75.4 137.6 %shard_map.102 = (bf16[768,1024]{1,0:T(8,128)(2,1)S(1)}, bf16[768,1024]{1,0:T(8,128)(2,1)S(1)}, bf16[4,1024,256]{2,1,0:T(8,128)(2,1)}, bf16[256,4096]{1,0:T(8,128)(2,1)}) custom-call(bf16[768,1024]{1,0:T(8,128)(2,1)S(1)} %get-tuple-element.36.tok_ref, bf16[768,1024]{1,0:T(8,128)(2,1)} %get-tuple-element.35.cot_ref, ...), custom_call_target="tpu_custom_call" | custom-call | tf_op jit(solution)/shard_map/pallas_call | solution.py:394
  213.0 1.6 gather_fusion.2
  215.2 2.2 multiply_reduce_fusion.1
  217.4 0.6 broadcast_in_dim.64.refs_2_
  218.0 59.1 %shard_map.103 = (bf16[4,32,4096]{2,1,0:T(8,128)(2,1)}, bf16[4,32,4096]{2,1,0:T(8,128)(2,1)}, f32[16,8,256]{2,1,0:T(8,128)}, bf16[4096,256]{1,0:T(8,128)(2,1)}) custom-call(bf16[16,32,1024]{2,1,0:T(8,128)(2,1)} %gather_fusion.2, bf16[16,32,1024]{2,1,0:T(8,128)(2,1)} %copy-done.1, f32[4,8,256]{2,1,0:T(8,128)} %broadcast_in_dim.64.refs_2_, ...), custom_call_target="tpu_custom_call" | custom-call | tf_op jit(solution)/shard_map/pallas_call | solution.py:119
  277.1 1.9 multiply_reduce_fusion
  279.0 1.0 slice_reduce_fusion.1
  281.3 2.2 fusion.6
  283.6 1.3 copy.16
  284.9 1.0 copy-done.4
  285.9 1.3 copy.17
  (35 shorter events, 2.8 us)
Async XLA Ops:
  215.2 2.8 copy-start.1
  218.0 59.1 %copy-start = (bf16[1,128,4096]{2,1,0:T(8,128)(2,1)S(1)}, bf16[1,128,4096]{2,1,0:T(8,128)(2,1)}, u32[]{:S(2)}) copy-start(bf16[1,128,4096]{2,1,0:T(8,128)(2,1)} %param.6) | copy-start | bytes 3145732
  277.1 3.6 %copy-start.2 = (bf16[4,32,4096]{2,1,0:T(8,128)(2,1)S(1)}, bf16[4,32,4096]{2,1,0:T(8,128)(2,1)}, u32[]{:S(2)}) copy-start(bf16[4,32,4096]{2,1,0:T(8,128)(2,1)} %get-tuple-element.27) | copy-start | bytes 3145732
  278.9 2.0 copy-start.3
  280.1 1.3 copy-start.6
  281.3 2.2 copy-start.5
  283.6 2.3 copy-start.4
